TPU v7x, 32 devices: a whole 2x2x4 slice. The times are simulated.
32 devices in a mesh: tm: 16 (over z, x, core), dish: 2 (over y).
Axes of the slice: x: 2, y: 2, z: 4, core: 2. Of those that a mesh axis runs over, the one named last changes fastest.
Arguments:
- voltages: bfloat16 [2, 64, 65536], P(None, 'dish', 'tm'), may hold values from -6 to 6
- beam_weights: bfloat16 [2, 64], P(None, 'dish'), may hold values from -0.75 to 0.75
- phase_bins: int32 [65536], P('tm'), may hold values from 0 to 1023, as said below
Outputs:
- spectrum: float32 [2048, 2, 1024], P('dish', None, 'tm')
Inputs may be any that keep to these rules, and one draw needn't show every extreme that they name: `phase_bins`: from each time sample to the next the bin stays or advances by one, wrapping from 1023 to 0; every bin occurs.
All inputs are finite; a program needn't handle non-finite values.
Results may differ from a plain program's by a relative error of at most 0.0039.
Values may be sent and summed in bfloat16 or wider, within the bound.
A program may use at most 128 MiB of HBM per device.

v0:
```python
import math

import jax
import jax.numpy as jnp
from jax import lax
from jax.sharding import PartitionSpec as P

PH = 1024
LAGS = 2048


def from_behind(value, axis, steps):
    count = lax.axis_size(axis)
    first, last = (max(0, -steps), min(count, count - steps))
    return lax.ppermute(value, axis, [(source, source + steps) for source in range(first, last)])


def form_beam(volt_block, weights):
    dish_count = volt_block.shape[1]
    mixer_rows = jnp.stack(
        [jnp.concatenate([weights[0], -weights[1]]), jnp.concatenate([weights[1], weights[0]])]
    )
    flat_volts = volt_block.reshape(2 * dish_count, volt_block.shape[2])
    return jnp.dot(mixer_rows, flat_volts, preferred_element_type=jnp.float32)


def hankel_rows(segment, row_count, lag_count):
    span_width = row_count + lag_count
    tiled_rows = jnp.broadcast_to(segment[:, None, :], (2, row_count + 1, span_width)).reshape(
        2, (row_count + 1) * span_width
    )
    return tiled_rows[:, : row_count * (span_width + 1)].reshape(2, row_count, span_width + 1)[
        :, :, :lag_count
    ]


def fold_block(extended, phase_bins, row_start, lag_start, row_count, lag_count, targets):
    current = lax.dynamic_slice_in_dim(extended, row_start, row_count, 1)
    segment = lax.dynamic_slice_in_dim(extended, row_start + lag_start, row_count + lag_count, 1)
    hankel = hankel_rows(segment, row_count, lag_count)
    upper_half = jnp.concatenate([hankel[0], hankel[1]], 1)
    lower_half = jnp.concatenate([hankel[1], -hankel[0]], 1)
    right_side = jnp.concatenate([upper_half, lower_half], 0)
    bin_block = lax.dynamic_slice_in_dim(phase_bins, row_start, row_count)
    select = (targets[:, None] == bin_block[None, :]).astype(jnp.bfloat16)
    left_side = jnp.concatenate([select * current[0][None, :], select * current[1][None, :]], 1)
    return jnp.dot(left_side, right_side, preferred_element_type=jnp.float32)


def transform_rows(coeffs, row_count, lag_start, lag_count, spectral_scale):
    frequency = jnp.arange(row_count, dtype=jnp.int32)
    lag_index = lag_start + jnp.arange(lag_count, dtype=jnp.int32)
    turn_index = frequency[:, None] * lag_index[None, :] % LAGS
    phase_angle = turn_index.astype(jnp.float32) * (2.0 * math.pi / LAGS)
    cosine = jnp.cos(phase_angle)
    sine_table = jnp.sin(phase_angle)
    left_side = jnp.concatenate(
        [jnp.concatenate([cosine, sine_table], 1), jnp.concatenate([-sine_table, cosine], 1)], 0
    )
    product = lax.dot_general(
        left_side,
        coeffs,
        (((1,), (1,)), ((), ())),
        precision=lax.Precision.HIGHEST,
        preferred_element_type=jnp.float32,
    )
    return jnp.transpose(product.reshape(2, row_count, coeffs.shape[0]), (1, 0, 2)) * spectral_scale


def per_device(voltages, beam_weights, phase_bins):
    samples = phase_bins.shape[0]
    count_tm = lax.axis_size("tm")
    count_dish = lax.axis_size("dish")
    dish_index = lax.axis_index("dish")
    rim_volts = from_behind(voltages[:, :, :LAGS], "tm", -1)
    partial_value = form_beam(jnp.concatenate([voltages, rim_volts], 2), beam_weights)
    extended = lax.psum(partial_value, "dish").astype(jnp.bfloat16)
    spectral_scale = 1.0 / math.sqrt(LAGS * samples * count_tm / PH)
    block_rows = min(512, samples)
    lag_share = LAGS // count_dish
    lag_start = dish_index * lag_share
    targets = jnp.arange(PH, dtype=jnp.int32)

    def accumulate(block_step, running):
        return running + fold_block(
            extended, phase_bins, block_step * block_rows, lag_start, block_rows, lag_share, targets
        )

    folded = lax.fori_loop(
        0, samples // block_rows, accumulate, jnp.zeros((PH, 2 * lag_share), jnp.float32)
    )
    owned_fold = lax.psum_scatter(folded, "tm", scatter_dimension=0, tiled=True)
    return lax.psum_scatter(
        transform_rows(
            owned_fold, lag_share * lax.axis_size("dish"), lag_start, lag_share, spectral_scale
        ),
        "dish",
        scatter_dimension=0,
        tiled=True,
    )


def solution(mesh):
    return jax.shard_map(
        per_device,
        mesh=mesh,
        in_specs=(P(None, "dish", "tm"), P(None, "dish"), P("tm")),
        out_specs=P("dish", None, "tm"),
        check_vma=False,
    )
```

profile of v0, /device:TPU:0, one launch (start us, length us, event | category | flops | bytes accessed | tf_op | source)
XLA Modules:
  0.0 539.1 jit_solution(15703736862105882621)
XLA Ops:
  12.2 10.2 %psum.7 = bf16[2,6144]{1,0:T(2,128)(2,1)S(1)} all-reduce(f32[2,6144]{1,0:T(2,128)S(1)} %fusion.39), channel_id=1, replica_groups=mesh['tm'=16,'dish'=2] {'dish'}, use_global_device_ids=true, to_apply=%region_0.0 | all-reduce | flops 12288 | bytes 73728 | tf_op jit(solution)/shard_map/psum | solution.py:77
  22.4 335.9 %while.14 = (s32[]{:T(128)}, f32[1024,2048]{1,0:T(8,128)}, s32[4096]{0:T(1024)}, bf16[2,6144]{1,0:T(2,128)(2,1)S(1)}, s32[]{:T(128)}, /*index=5*/s32[]{:T(128)},...) while((s32[]{:T(128)}, f32[1024,2048]{1,0:T(8,128)}, s32[4096]{0:T(1024)}, ...), condition=%wide.region_2.0_spmd.clone, body=%wide.region_1.0_spmd.clone.sunk | while | flops 4322230272 | bytes 58781964 | solution.py:89
  33.8 7.4 %reshape.37 = bf16[2,512,1537]{2,1,0:T(8,128)(2,1)S(1)} reshape(bf16[1573888]{0:T(1024)(128)(2,1)} %reshape.36) | data formatting | bytes 6295552 | tf_op jit(solution)/shard_map/while/body/eval_jaxpr/reshape | solution.py:32
  41.6 21.8 %select_add_fusion.2 = f32[1024,2048]{1,0:T(8,128)} fusion(f32[1024,2048]{1,0:T(8,128)} %get-tuple-element.213, pred[]{:T(512)S(6)} %compare.4, bf16[512,1024]{1,0:T(8,128)(2,1)S(1)} %fusion.54, bf16[512,1024]{1,0:T(8,128)(2,1)S(1)} %get-tuple-element.195, bf16[512,1024]{1,0:T(8,128)(2,1)S(1)} %get-tuple-element.196, ...), kind=kOutput, calls=%fused_computation.1.clone.1 | convolution fusion | flops 4320133120 | bytes 22020096 | tf_op jit(solution)/shard_map/while/body/eval_jaxpr/dot_general | solution.py:47
  71.0 3.7 reshape.36
  74.7 7.4 %reshape.37 = bf16[2,512,1537]{2,1,0:T(8,128)(2,1)S(1)} reshape(bf16[1573888]{0:T(1024)(128)(2,1)} %reshape.36) | data formatting | bytes 6295552 | tf_op jit(solution)/shard_map/while/body/eval_jaxpr/reshape | solution.py:32
  82.5 23.0 %select_add_fusion.2 = f32[1024,2048]{1,0:T(8,128)} fusion(f32[1024,2048]{1,0:T(8,128)} %get-tuple-element.213, pred[]{:T(512)S(6)} %compare.4, bf16[512,1024]{1,0:T(8,128)(2,1)S(1)} %fusion.54, bf16[512,1024]{1,0:T(8,128)(2,1)S(1)} %get-tuple-element.195, bf16[512,1024]{1,0:T(8,128)(2,1)S(1)} %get-tuple-element.196, ...), kind=kOutput, calls=%fused_computation.1.clone.1 | convolution fusion | flops 4320133120 | bytes 22020096 | tf_op jit(solution)/shard_map/while/body/eval_jaxpr/dot_general | solution.py:47
  116.8 7.4 %reshape.37 = bf16[2,512,1537]{2,1,0:T(8,128)(2,1)S(1)} reshape(bf16[1573888]{0:T(1024)(128)(2,1)} %reshape.36) | data formatting | bytes 6295552 | tf_op jit(solution)/shard_map/while/body/eval_jaxpr/reshape | solution.py:32
  124.6 23.0 %select_add_fusion.2 = f32[1024,2048]{1,0:T(8,128)} fusion(f32[1024,2048]{1,0:T(8,128)} %get-tuple-element.213, pred[]{:T(512)S(6)} %compare.4, bf16[512,1024]{1,0:T(8,128)(2,1)S(1)} %fusion.54, bf16[512,1024]{1,0:T(8,128)(2,1)S(1)} %get-tuple-element.195, bf16[512,1024]{1,0:T(8,128)(2,1)S(1)} %get-tuple-element.196, ...), kind=kOutput, calls=%fused_computation.1.clone.1 | convolution fusion | flops 4320133120 | bytes 22020096 | tf_op jit(solution)/shard_map/while/body/eval_jaxpr/dot_general | solution.py:47
  159.0 7.4 %reshape.37 = bf16[2,512,1537]{2,1,0:T(8,128)(2,1)S(1)} reshape(bf16[1573888]{0:T(1024)(128)(2,1)} %reshape.36) | data formatting | bytes 6295552 | tf_op jit(solution)/shard_map/while/body/eval_jaxpr/reshape | solution.py:32
  166.8 23.0 %select_add_fusion.2 = f32[1024,2048]{1,0:T(8,128)} fusion(f32[1024,2048]{1,0:T(8,128)} %get-tuple-element.213, pred[]{:T(512)S(6)} %compare.4, bf16[512,1024]{1,0:T(8,128)(2,1)S(1)} %fusion.54, bf16[512,1024]{1,0:T(8,128)(2,1)S(1)} %get-tuple-element.195, bf16[512,1024]{1,0:T(8,128)(2,1)S(1)} %get-tuple-element.196, ...), kind=kOutput, calls=%fused_computation.1.clone.1 | convolution fusion | flops 4320133120 | bytes 22020096 | tf_op jit(solution)/shard_map/while/body/eval_jaxpr/dot_general | solution.py:47
  197.5 3.7 reshape.36
  201.1 7.4 %reshape.37 = bf16[2,512,1537]{2,1,0:T(8,128)(2,1)S(1)} reshape(bf16[1573888]{0:T(1024)(128)(2,1)} %reshape.36) | data formatting | bytes 6295552 | tf_op jit(solution)/shard_map/while/body/eval_jaxpr/reshape | solution.py:32
  208.9 23.0 %select_add_fusion.2 = f32[1024,2048]{1,0:T(8,128)} fusion(f32[1024,2048]{1,0:T(8,128)} %get-tuple-element.213, pred[]{:T(512)S(6)} %compare.4, bf16[512,1024]{1,0:T(8,128)(2,1)S(1)} %fusion.54, bf16[512,1024]{1,0:T(8,128)(2,1)S(1)} %get-tuple-element.195, bf16[512,1024]{1,0:T(8,128)(2,1)S(1)} %get-tuple-element.196, ...), kind=kOutput, calls=%fused_computation.1.clone.1 | convolution fusion | flops 4320133120 | bytes 22020096 | tf_op jit(solution)/shard_map/while/body/eval_jaxpr/dot_general | solution.py:47
  243.2 7.4 %reshape.37 = bf16[2,512,1537]{2,1,0:T(8,128)(2,1)S(1)} reshape(bf16[1573888]{0:T(1024)(128)(2,1)} %reshape.36) | data formatting | bytes 6295552 | tf_op jit(solution)/shard_map/while/body/eval_jaxpr/reshape | solution.py:32
  251.0 23.0 %select_add_fusion.2 = f32[1024,2048]{1,0:T(8,128)} fusion(f32[1024,2048]{1,0:T(8,128)} %get-tuple-element.213, pred[]{:T(512)S(6)} %compare.4, bf16[512,1024]{1,0:T(8,128)(2,1)S(1)} %fusion.54, bf16[512,1024]{1,0:T(8,128)(2,1)S(1)} %get-tuple-element.195, bf16[512,1024]{1,0:T(8,128)(2,1)S(1)} %get-tuple-element.196, ...), kind=kOutput, calls=%fused_computation.1.clone.1 | convolution fusion | flops 4320133120 | bytes 22020096 | tf_op jit(solution)/shard_map/while/body/eval_jaxpr/dot_general | solution.py:47
  285.4 7.4 %reshape.37 = bf16[2,512,1537]{2,1,0:T(8,128)(2,1)S(1)} reshape(bf16[1573888]{0:T(1024)(128)(2,1)} %reshape.36) | data formatting | bytes 6295552 | tf_op jit(solution)/shard_map/while/body/eval_jaxpr/reshape | solution.py:32
  293.2 23.0 %select_add_fusion.2 = f32[1024,2048]{1,0:T(8,128)} fusion(f32[1024,2048]{1,0:T(8,128)} %get-tuple-element.213, pred[]{:T(512)S(6)} %compare.4, bf16[512,1024]{1,0:T(8,128)(2,1)S(1)} %fusion.54, bf16[512,1024]{1,0:T(8,128)(2,1)S(1)} %get-tuple-element.195, bf16[512,1024]{1,0:T(8,128)(2,1)S(1)} %get-tuple-element.196, ...), kind=kOutput, calls=%fused_computation.1.clone.1 | convolution fusion | flops 4320133120 | bytes 22020096 | tf_op jit(solution)/shard_map/while/body/eval_jaxpr/dot_general | solution.py:47
  327.5 7.4 %reshape.37 = bf16[2,512,1537]{2,1,0:T(8,128)(2,1)S(1)} reshape(bf16[1573888]{0:T(1024)(128)(2,1)} %reshape.36) | data formatting | bytes 6295552 | tf_op jit(solution)/shard_map/while/body/eval_jaxpr/reshape | solution.py:32
  335.3 23.0 %select_add_fusion.2 = f32[1024,2048]{1,0:T(8,128)} fusion(f32[1024,2048]{1,0:T(8,128)} %get-tuple-element.213, pred[]{:T(512)S(6)} %compare.4, bf16[512,1024]{1,0:T(8,128)(2,1)S(1)} %fusion.54, bf16[512,1024]{1,0:T(8,128)(2,1)S(1)} %get-tuple-element.195, bf16[512,1024]{1,0:T(8,128)(2,1)S(1)} %get-tuple-element.196, ...), kind=kOutput, calls=%fused_computation.1.clone.1 | convolution fusion | flops 4320133120 | bytes 22020096 | tf_op jit(solution)/shard_map/while/body/eval_jaxpr/dot_general | solution.py:47
  358.4 37.3 %fusion.36 = (f32[2048,1024]{1,0:T(8,128)}, f32[2048,1024]{1,0:T(8,128)}, f32[2048,1024]{1,0:T(8,128)}) fusion(s32[1024]{0:T(1024)S(1)} %iota_add_fusion), kind=kLoop, calls=%fused_computation.42 | loop fusion | flops 31457280 | bytes 25169920 | tf_op jit(solution)/shard_map/sin | solution.py:56
  395.7 70.1 %reduce-scatter.3.cloned.1.call-done = f32[64,2048]{1,0:T(8,128)} async-done(((f32[1024,2048]{1,0:T(8,128)}), f32[64,2048]{1,0:T(8,128)}) %reduce-scatter.3.cloned.1.call-update) | async-done | bytes 524304 | tf_op jit(solution)/shard_map/reduce_scatter | solution.py:92
  465.8 45.1 %fusion.33 = f32[4096,64]{0,1:T(8,128)S(1)} fusion(f32[64,2048]{1,0:T(8,128)} %reduce-scatter.3.cloned.1.call-done, f32[2048,1024]{1,0:T(8,128)} %get-tuple-element.153, f32[2048,1024]{1,0:T(8,128)} %get-tuple-element.152, f32[2048,1024]{1,0:T(8,128)} %get-tuple-element.151), kind=kOutput, calls=%fused_computation.41 | convolution fusion | flops 6467878912 | bytes 26738688 | tf_op jit(solution)/shard_map/dot_general | solution.py:60
  512.0 20.2 %reduce-scatter.5.cloned.1.call-done = f32[1024,2,64]{0,2,1:T(8,128)} async-done(((f32[2048,2,64]{0,2,1:T(8,128)}), f32[1024,2,64]{0,2,1:T(8,128)}) %reduce-scatter.5.cloned.1.call-update) | async-done | bytes 524304 | tf_op jit(solution)/shard_map/reduce_scatter | solution.py:93
  (93 shorter events, 92.7 us)
Async XLA Ops:
  6.5 459.3 %reduce-scatter.3.cloned.1.call-start = ((), (), s32[]{:S(2)}) async-start(), calls=%async_computation.2 | async-start | bytes 8912896 | tf_op jit(solution)/shard_map/reduce_scatter | solution.py:92
  7.5 3.4 collective-permute-start
  358.4 173.9 %reduce-scatter.5.cloned.1.call-start = ((), (), s32[]{:S(2)}) async-start(), calls=%async_computation.3 | async-start | bytes 1572864 | tf_op jit(solution)/shard_map/reduce_scatter | solution.py:93
Sparse Core Ops, SparseCore 0:
  358.5 107.3 reduce-scatter.2
  512.2 20.0 reduce-scatter.4
where the time goes:
time: 540 us; the launch traced here: 539 us
  matrix products  228 us (42%)
  local copies, waits for them, and re-layouts  140 us (26%)
  waiting for transfers between devices  91 us (17%)
  other arithmetic  54.2 us (10%)
  between operations  13.5 us (2%)
  blocking collectives  10.2 us (2%)
    dot_general x8, matrix products, fold_block(): return jnp.dot(left_side, right_side, preferred_element_type=jnp.float32)  183 us
    reduce_scatter x1, waiting for transfers between devices, per_device(): owned_fold = lax.psum_scatter(folded, 'tm', scatter_dimension=0, tiled=True)  70.1 us
    reshape x8, local copies, waits for them, and re-layouts, hankel_rows(): tiled_rows[:, :row_count * (span_width + 1)]  59.3 us
    while x24, local copies, waits for them, and re-layouts  50.4 us
    dot_general x1, matrix products, transform_rows(): lax.dot_general(left_side, coeffs, (((1,), (1,)), ((), ())), precision=la...  45.1 us
    sin x1, other arithmetic, transform_rows(): sine_table = jnp.sin(phase_angle)  37.3 us
    reduce_scatter x1, waiting for transfers between devices, per_device(): lax.psum_scatter(transform_rows(owned_fold, lag_share * lax.axis_size('di...  20.2 us
    slice x8, local copies, waits for them, and re-layouts, hankel_rows(): tiled_rows[:, :row_count * (span_width + 1)]  18.6 us
  transfers between devices with their start and end apart: 3, of which 3 were waited for; matrix products, arithmetic and copies ran while one was open for 7% of the time, Pallas kernels for 0%

commit v1 on v0

v1 whole, which is shorter than its diff:
```python
import functools
import math

import jax
import jax.numpy as jnp
import ml_dtypes
import numpy as np
from jax import lax
from jax.experimental import pallas as pl
from jax.experimental.pallas import tpu as pltpu
from jax.sharding import PartitionSpec as P

PH = 1024
LAGS = 2048
BLOCK = 128
GROUP = 16
LAG_PIECE = 512


def form_beam(volt_block, weights):
    dish_count = volt_block.shape[1]
    mixer_rows = jnp.stack(
        [jnp.concatenate([weights[0], -weights[1]]), jnp.concatenate([weights[1], weights[0]])]
    )
    flat_volts = volt_block.reshape(2 * dish_count, volt_block.shape[2])
    return jnp.dot(mixer_rows, flat_volts, preferred_element_type=jnp.float32)


def fold_kernel(chunk, bin_count, list_ref, count_ref, base_ref, beam_ref, bins_ref, out_ref, shifted, hankel):
    step = pl.program_id(0)
    start = pl.multiple_of(step * chunk, BLOCK)
    width = chunk + LAGS
    blocks_here = chunk // BLOCK

    @pl.when(step == 0)
    def _():
        out_ref[...] = jnp.zeros_like(out_ref)

    count = count_ref[step]

    @pl.when(count > 0)
    def _():
        row = lax.broadcasted_iota(jnp.int32, (GROUP, 2 * BLOCK), 0)

        def shift_rows(position, carry):
            lane = pl.multiple_of(position * BLOCK, BLOCK)
            for part in range(2):
                rows = jnp.broadcast_to(
                    beam_ref[pl.ds(part, 1), pl.ds(pl.multiple_of(start + lane, BLOCK), 2 * BLOCK)],
                    (GROUP, 2 * BLOCK),
                )
                amount = 1
                while amount < GROUP:
                    rows = jnp.where(
                        (row & amount) != 0, pltpu.roll(rows, 2 * BLOCK - amount, 1), rows
                    )
                    amount *= 2
                shifted[part, :, pl.ds(lane, BLOCK)] = rows[:, :BLOCK]
            return carry

        lax.fori_loop(0, width // BLOCK, shift_rows, 0)
        lane_index = lax.broadcasted_iota(jnp.int32, (GROUP, BLOCK), 1)

        def build(position, carry):
            lane = pl.multiple_of(position * BLOCK, BLOCK)
            for part in range(2):
                near = shifted[part, :, pl.ds(lane, BLOCK)]
                far = shifted[part, :, pl.ds(lane + BLOCK, BLOCK)]
                for group in range(BLOCK // GROUP):
                    offset = group * GROUP
                    if offset == 0:
                        piece = near
                    else:
                        mixed = jnp.where(lane_index < offset, far, near)
                        piece = pltpu.roll(mixed, BLOCK - offset, 1)
                    hankel[pl.ds(pl.multiple_of(lane + offset, GROUP), GROUP), pl.ds(part * BLOCK, BLOCK)] = (
                        piece.astype(jnp.bfloat16)
                    )
            return carry

        lax.fori_loop(0, width // BLOCK - 1, build, 0)
        target = base_ref[0] + lax.broadcasted_iota(jnp.int32, (bin_count, BLOCK), 0)

        def fold(position, carry):
            row_start = pl.multiple_of(list_ref[step * blocks_here + position] * BLOCK, BLOCK)
            lane = pl.ds(pl.multiple_of(start + row_start, BLOCK), BLOCK)
            real = beam_ref[0:1, lane]
            imag = beam_ref[1:2, lane]
            chosen = bins_ref[0:1, lane] == target
            zero = jnp.zeros((bin_count, BLOCK), jnp.float32)
            chosen_real = jnp.where(chosen, real, zero)
            chosen_imag = jnp.where(chosen, imag, zero)
            right = jnp.concatenate(
                [
                    jnp.concatenate([chosen_real, chosen_imag], 1),
                    jnp.concatenate([-chosen_imag, chosen_real], 1),
                ],
                0,
            ).astype(jnp.bfloat16)
            for piece in range(LAGS // LAG_PIECE):
                rows = pl.ds(piece * LAG_PIECE, LAG_PIECE)
                left = hankel[pl.ds(pl.multiple_of(row_start + piece * LAG_PIECE, BLOCK), LAG_PIECE), :]
                out_ref[rows, :] += lax.dot_general(
                    left, right, (((1,), (1,)), ((), ())), preferred_element_type=jnp.float32
                )
            return carry

        lax.fori_loop(0, count, fold, 0)


def transform_table(row_count):
    turn = np.arange(row_count)[:, None] * np.arange(LAGS)[None, :] % LAGS
    angle = turn * (2.0 * math.pi / LAGS)
    return np.concatenate([np.cos(angle), np.sin(angle)], 0).astype(ml_dtypes.bfloat16)


def per_device(table, voltages, beam_weights, phase_bins):
    samples = phase_bins.shape[0]
    count_tm = lax.axis_size("tm")
    count_dish = lax.axis_size("dish")
    total = samples * count_tm
    own_bins = PH // count_tm
    bin_count = max(own_bins, 64)
    base = lax.axis_index("tm") * own_bins
    all_bins = lax.all_gather(phase_bins, "tm", axis=0, tiled=True)
    beam = lax.psum(form_beam(voltages, beam_weights), "dish").astype(jnp.bfloat16)
    beam = lax.all_gather(beam, "tm", axis=1, tiled=True)
    beam = jnp.pad(beam.astype(jnp.float32), ((0, 0), (0, LAGS + BLOCK)))

    chunk = min(16384, total)
    steps = total // chunk
    here = chunk // BLOCK
    inside = (all_bins >= base) & (all_bins < base + own_bins)
    touched = jnp.any(inside.reshape(steps, here, BLOCK), axis=2)
    number = jnp.arange(here, dtype=jnp.int32)
    before = jnp.sum(touched[:, None, :] & (number[None, None, :] < number[None, :, None]), 2, dtype=jnp.int32)
    counts = jnp.sum(touched, 1, dtype=jnp.int32)
    hit = touched[:, None, :] & (before[:, None, :] == number[None, :, None])
    listed = jnp.sum(jnp.where(hit, number[None, None, :], 0), 2, dtype=jnp.int32)

    folded = pl.pallas_call(
        functools.partial(fold_kernel, chunk, bin_count),
        grid=(steps,),
        out_shape=jax.ShapeDtypeStruct((LAGS, 2 * bin_count), jnp.float32),
        in_specs=[pl.BlockSpec(memory_space=pltpu.SMEM)] * 3 + [pl.BlockSpec(memory_space=pltpu.VMEM)] * 2,
        out_specs=pl.BlockSpec((LAGS, 2 * bin_count), lambda step: (0, 0)),
        scratch_shapes=[
            pltpu.VMEM((2, GROUP, chunk + LAGS), jnp.float32),
            pltpu.VMEM((chunk + LAGS - BLOCK, 2 * BLOCK), jnp.bfloat16),
        ],
        compiler_params=pltpu.CompilerParams(vmem_limit_bytes=48 * 2**20),
    )(listed.reshape(-1), counts, base.reshape(1), beam, all_bins.reshape(1, total))

    real = folded[:, :own_bins]
    imag = folded[:, bin_count : bin_count + own_bins]
    turn = (lax.axis_index("dish") * jnp.arange(LAGS, dtype=jnp.int32) % count_dish).astype(jnp.float32)
    angle = turn * (2.0 * math.pi / count_dish)
    cosine, sine = jnp.cos(angle)[:, None], jnp.sin(angle)[:, None]
    coeffs = jnp.concatenate([real * cosine + imag * sine, imag * cosine - real * sine], 1)
    high = lax.reduce_precision(coeffs, 8, 7)
    split = jnp.concatenate([high, coeffs - high], 1).astype(jnp.bfloat16)
    product = jnp.dot(table, split, preferred_element_type=jnp.float32)
    product = product[:, : 2 * own_bins] + product[:, 2 * own_bins :]
    rows = LAGS // count_dish
    by_cosine, by_sine = product[:rows], product[rows:]
    scale = 1.0 / math.sqrt(LAGS * total / PH)
    out_real = by_cosine[:, :own_bins] + by_sine[:, own_bins:]
    out_imag = by_cosine[:, own_bins:] - by_sine[:, :own_bins]
    return jnp.stack([out_real, out_imag], 1) * scale


def solution(mesh):
    table = transform_table(LAGS // mesh.shape["dish"])

    def run(voltages, beam_weights, phase_bins):
        return jax.shard_map(
            functools.partial(per_device, jnp.asarray(table)),
            mesh=mesh,
            in_specs=(P(None, "dish", "tm"), P(None, "dish"), P("tm")),
            out_specs=P("dish", None, "tm"),
            check_vma=False,
        )(voltages, beam_weights, phase_bins)

    return run
```

time: 540 us -> 303 us (0.56)
  Pallas kernels: 0 us -> 244 us
  matrix products: 228 us -> 2.54 us
  local copies, waits for them, and re-layouts: 140 us -> 1.78 us
  waiting for transfers between devices: 91 us -> 0 us
  other arithmetic: 54.2 us -> 4.03 us
  blocking collectives: 10.2 us -> 50.5 us
  between operations: 13.5 us -> 0.09 us
    pallas_call x0 -> x1, Pallas kernels: none -> 244 us  [per_device(): pl.pallas_call(functools.partial(fold_kernel, chunk, bin_count), grid=(st...]
    dot_general x9 -> x1, matrix products: 228 us -> 2.36 us  [per_device(): product = jnp.dot(table, split, preferred_element_type=jnp.float32)]
    reduce_scatter x2 -> x0, waiting for transfers between devices: 90.4 us -> none  [the longest x1 70.1 us: per_device(): owned_fold = lax.psum_scatter(folded, 'tm', scatter_dimension=0, tiled=True)]
    reshape x8 -> x0, local copies, waits for them, and re-layouts: 59.3 us -> none  [hankel_rows(): tiled_rows[:, :row_count * (span_width + 1)]]
    while x24 -> x0, local copies, waits for them, and re-layouts: 50.4 us -> none
    all_gather x0 -> x2, blocking collectives: none -> 40.6 us  [the longest x1 22.2 us: per_device(): beam = lax.all_gather(beam, 'tm', axis=1, tiled=True)]
    sin x1, other arithmetic: 37.3 us -> 0.06 us  [per_device(): cosine, sine = (jnp.cos(angle)[:, None], jnp.sin(angle)[:, None])]
    slice x17 -> x0, local copies, waits for them, and re-layouts: 20.4 us -> none  [the longest x8 18.6 us: hankel_rows(): tiled_rows[:, :row_count * (span_width + 1)]]
  transfers between devices with their start and end apart: 3 -> 0, of which waited for: 3 -> 0; matrix products, arithmetic and copies ran while one was open for 7% -> 0% of each run, Pallas kernels for 0% -> 0%
where the time goes in v1:
time: 303 us
  Pallas kernels  244 us (81%)
  blocking collectives  50.5 us (17%)
  other arithmetic  4.03 us (1%)
    pallas_call x1, Pallas kernels, per_device(): pl.pallas_call(functools.partial(fold_kernel, chunk, bin_count), grid=(st...  244 us
    all_gather x1, blocking collectives, per_device(): beam = lax.all_gather(beam, 'tm', axis=1, tiled=True)  22.2 us
    all_gather x1, blocking collectives, per_device(): all_bins = lax.all_gather(phase_bins, 'tm', axis=0, tiled=True)  18.4 us
    psum x1, blocking collectives, per_device(): lax.psum(form_beam(voltages, beam_weights), 'dish').astype(jnp.bfloat16)  9.95 us

profile of v1, /device:TPU:0, one launch (start us, length us, event | category | flops | bytes accessed | tf_op | source)
XLA Modules:
  0.0 302.8 jit_solution(15626456806060428755)
XLA Ops:
  0.0 0.0 copy-start
  0.0 1.0 copy-done
  1.0 0.7 fusion.19
  1.7 0.7 slice_bitcast_fusion
  2.4 0.1 maximum_bitcast_fusion
  2.5 0.1 fusion.11
  2.6 0.2 fusion.13
  2.8 10.0 %psum.7 = bf16[2,4096]{1,0:T(2,128)(2,1)S(1)} all-reduce(f32[2,4096]{1,0:T(2,128)S(1)} %fusion.13), channel_id=1, replica_groups=mesh['tm'=16,'dish'=2] {'dish'}, use_global_device_ids=true, to_apply=%region_4.5 | all-reduce | flops 8192 | bytes 49152 | tf_op jit(solution)/shard_map/psum | solution.py:126
  12.7 22.2 %all_gather.7 = bf16[2,65536]{1,0:T(2,128)(2,1)S(1)} all-gather(bf16[2,4096]{1,0:T(2,128)(2,1)S(1)} %psum.7), channel_id=1, replica_groups=mesh['tm'=16,'dish'=2] {'tm'}, dimensions={1}, use_global_device_ids=true | all-gather | bytes 278528 | tf_op jit(solution)/shard_map/all_gather | solution.py:127
  34.9 18.4 %all_gather.6 = s32[65536]{0:T(1024)S(1)} all-gather(s32[4096]{0:T(1024)} %param.6), channel_id=1, replica_groups=mesh['tm'=16,'dish'=2] {'tm'}, dimensions={0}, use_global_device_ids=true | all-gather | bytes 278528 | tf_op jit(solution)/shard_map/all_gather | solution.py:125
  53.3 0.1 compare_and_fusion
  53.4 0.1 reduce_or.9
  53.5 0.2 convert_reduce_fusion
  53.7 0.1 select_reduce_fusion
  53.8 0.1 convert_reduce_fusion.1.count_ref
  53.9 0.2 pad_convert_fusion.beam_ref
  54.2 0.0 copy-start.1
  54.2 243.8 %shard_map.46 = f32[2048,128]{1,0:T(8,128)S(1)} custom-call(s32[512]{0:T(512)S(1)} %bitcast.23, s32[4]{0:T(128)S(1)} %convert_reduce_fusion.1.count_ref, s32[1]{0:T(128)} %bitcast.2.base_ref, f32[2,67712]{1,0:T(2,128)S(1)} %pad_convert_fusion.beam_ref, s32[1,65536]{1,0:T(1,128)S(1)} %bitcast.22), custom_call_target="tpu_custom_call" | custom-call | tf_op jit(solution)/shard_map/pallas_call | solution.py:141
  298.0 1.0 multiply_add_fusion
  299.0 0.3 reduce-precision_convert_fusion
  299.4 2.4 fusion.1
  301.7 0.1 slice_add_fusion
  301.9 0.1 fusion.3
  301.9 0.8 maximum_multiply_fusion
  (2 shorter events, 0.0 us)
Async XLA Ops:
  0.0 1.0 copy-start
  54.2 245.2 %copy-start.1 = (bf16[2048,2048]{1,0:T(8,128)(2,1)S(1)}, bf16[2048,2048]{1,0:T(8,128)(2,1)}, u32[]{:S(2)}) copy-start(bf16[2048,2048]{1,0:T(8,128)(2,1)} %constant.37.clone) | copy-start | bytes 25165828

commit v2 on v1

--- a/solution.py
+++ b/solution.py
@@ -15,6 +15,9 @@
 BLOCK = 128
 GROUP = 16
 LAG_PIECE = 512
+SPAN = 1024
+DIGIT = 32
+UNROLL = 4
 
 
 def form_beam(volt_block, weights):
@@ -40,45 +43,45 @@
 
     @pl.when(count > 0)
     def _():
-        row = lax.broadcasted_iota(jnp.int32, (GROUP, 2 * BLOCK), 0)
+        row = lax.broadcasted_iota(jnp.int32, (GROUP, SPAN + BLOCK), 0)
 
         def shift_rows(position, carry):
-            lane = pl.multiple_of(position * BLOCK, BLOCK)
+            lane = pl.multiple_of(position * SPAN, SPAN)
             for part in range(2):
                 rows = jnp.broadcast_to(
-                    beam_ref[pl.ds(part, 1), pl.ds(pl.multiple_of(start + lane, BLOCK), 2 * BLOCK)],
-                    (GROUP, 2 * BLOCK),
+                    beam_ref[pl.ds(part, 1), pl.ds(pl.multiple_of(start + lane, BLOCK), SPAN + BLOCK)],
+                    (GROUP, SPAN + BLOCK),
                 )
                 amount = 1
                 while amount < GROUP:
                     rows = jnp.where(
-                        (row & amount) != 0, pltpu.roll(rows, 2 * BLOCK - amount, 1), rows
+                        (row & amount) != 0, pltpu.roll(rows, SPAN + BLOCK - amount, 1), rows
                     )
                     amount *= 2
-                shifted[part, :, pl.ds(lane, BLOCK)] = rows[:, :BLOCK]
+                shifted[part, :, pl.ds(lane, SPAN)] = rows[:, :SPAN]
             return carry
 
-        lax.fori_loop(0, width // BLOCK, shift_rows, 0)
+        lax.fori_loop(0, width // SPAN, shift_rows, 0)
         lane_index = lax.broadcasted_iota(jnp.int32, (GROUP, BLOCK), 1)
 
         def build(position, carry):
-            lane = pl.multiple_of(position * BLOCK, BLOCK)
+            lane = pl.multiple_of(position * UNROLL * BLOCK, UNROLL * BLOCK)
             for part in range(2):
-                near = shifted[part, :, pl.ds(lane, BLOCK)]
-                far = shifted[part, :, pl.ds(lane + BLOCK, BLOCK)]
+                tiles = [
+                    shifted[part, :, pl.ds(lane + tile * BLOCK, BLOCK)] for tile in range(UNROLL + 1)
+                ]
                 for group in range(BLOCK // GROUP):
                     offset = group * GROUP
-                    if offset == 0:
-                        piece = near
-                    else:
-                        mixed = jnp.where(lane_index < offset, far, near)
-                        piece = pltpu.roll(mixed, BLOCK - offset, 1)
-                    hankel[pl.ds(pl.multiple_of(lane + offset, GROUP), GROUP), pl.ds(part * BLOCK, BLOCK)] = (
-                        piece.astype(jnp.bfloat16)
-                    )
+                    for tile in range(UNROLL):
+                        piece = tiles[tile]
+                        if offset > 0:
+                            mixed = jnp.where(lane_index < offset, tiles[tile + 1], piece)
+                            piece = pltpu.roll(mixed, BLOCK - offset, 1)
+                        first = pl.multiple_of(lane + tile * BLOCK + offset, GROUP)
+                        hankel[pl.ds(first, GROUP), pl.ds(part * BLOCK, BLOCK)] = piece.astype(jnp.bfloat16)
             return carry
 
-        lax.fori_loop(0, width // BLOCK - 1, build, 0)
+        lax.fori_loop(0, width // (UNROLL * BLOCK), build, 0)
         target = base_ref[0] + lax.broadcasted_iota(jnp.int32, (bin_count, BLOCK), 0)
 
         def fold(position, carry):
@@ -122,12 +125,14 @@
     own_bins = PH // count_tm
     bin_count = max(own_bins, 64)
     base = lax.axis_index("tm") * own_bins
-    all_bins = lax.all_gather(phase_bins, "tm", axis=0, tiled=True)
+    digits = jnp.stack([phase_bins // DIGIT, phase_bins % DIGIT]).astype(jnp.bfloat16)
     beam = lax.psum(form_beam(voltages, beam_weights), "dish").astype(jnp.bfloat16)
-    beam = lax.all_gather(beam, "tm", axis=1, tiled=True)
-    beam = jnp.pad(beam.astype(jnp.float32), ((0, 0), (0, LAGS + BLOCK)))
+    gathered = lax.all_gather(jnp.concatenate([beam, digits], 0), "tm", axis=1, tiled=True)
+    gathered = gathered.astype(jnp.float32)
+    beam = jnp.pad(gathered[:2], ((0, 0), (0, LAGS + BLOCK)))
+    all_bins = (gathered[2] * DIGIT + gathered[3]).astype(jnp.int32)
 
-    chunk = min(16384, total)
+    chunk = min(32768, total)
     steps = total // chunk
     here = chunk // BLOCK
     inside = (all_bins >= base) & (all_bins < base + own_bins)
@@ -145,8 +150,8 @@
         in_specs=[pl.BlockSpec(memory_space=pltpu.SMEM)] * 3 + [pl.BlockSpec(memory_space=pltpu.VMEM)] * 2,
         out_specs=pl.BlockSpec((LAGS, 2 * bin_count), lambda step: (0, 0)),
         scratch_shapes=[
-            pltpu.VMEM((2, GROUP, chunk + LAGS), jnp.float32),
-            pltpu.VMEM((chunk + LAGS - BLOCK, 2 * BLOCK), jnp.bfloat16),
+            pltpu.VMEM((2, GROUP, chunk + LAGS + BLOCK), jnp.float32),
+            pltpu.VMEM((chunk + LAGS, 2 * BLOCK), jnp.bfloat16),
         ],
         compiler_params=pltpu.CompilerParams(vmem_limit_bytes=48 * 2**20),
     )(listed.reshape(-1), counts, base.reshape(1), beam, all_bins.reshape(1, total))

time: 303 us -> 116 us (0.38)
  Pallas kernels: 244 us -> 71.9 us
  blocking collectives: 50.5 us -> 33.1 us
    pallas_call x1, Pallas kernels: 244 us -> 71.9 us  [per_device(): pl.pallas_call(functools.partial(fold_kernel, chunk, bin_count), grid=(st...]
    all_gather x2 -> x1, blocking collectives: 40.6 us -> 23.1 us  [per_device(): lax.all_gather(jnp.concatenate([beam, digits], 0), 'tm', axis=1, tiled=True)]
where the time goes in v2:
time: 116 us
  Pallas kernels  71.9 us (62%)
  blocking collectives  33.1 us (29%)
  other arithmetic  6.12 us (5%)
  matrix products  2.55 us (2%)
  local copies, waits for them, and re-layouts  2.13 us (2%)
    pallas_call x1, Pallas kernels, per_device(): pl.pallas_call(functools.partial(fold_kernel, chunk, bin_count), grid=(st...  71.9 us
    all_gather x1, blocking collectives, per_device(): lax.all_gather(jnp.concatenate([beam, digits], 0), 'tm', axis=1, tiled=True)  23.1 us
    psum x1, blocking collectives, per_device(): lax.psum(form_beam(voltages, beam_weights), 'dish').astype(jnp.bfloat16)  9.95 us
    dot_general x1, matrix products, per_device(): product = jnp.dot(table, split, preferred_element_type=jnp.float32)  2.37 us

profile of v2, /device:TPU:0, one launch (start us, length us, event | category | flops | bytes accessed | tf_op | source)
XLA Modules:
  0.0 115.9 jit_solution(162592096546690165)
XLA Ops:
  0.0 1.0 copy-done
  1.0 0.7 fusion.24
  1.7 0.7 slice_bitcast_fusion
  2.4 0.1 maximum_bitcast_fusion
  2.6 0.7 fusion.6
  3.4 0.2 fusion.18
  3.5 10.0 %psum.7 = bf16[2,4096]{1,0:T(2,128)(2,1)S(1)} all-reduce(f32[2,4096]{1,0:T(2,128)S(1)} %fusion.18), channel_id=1, replica_groups=mesh['tm'=16,'dish'=2] {'dish'}, use_global_device_ids=true, to_apply=%region_0.1 | all-reduce | flops 8192 | bytes 49152 | tf_op jit(solution)/shard_map/psum | solution.py:129
  13.5 0.1 pad_maximum_fusion.3
  13.6 23.1 %all_gather.3 = bf16[4,65536]{1,0:T(4,128)(2,1)S(1)} all-gather(bf16[4,4096]{1,0:T(4,128)(2,1)S(1)} %pad_maximum_fusion.3), channel_id=1, replica_groups=mesh['tm'=16,'dish'=2] {'tm'}, dimensions={1}, use_global_device_ids=true | all-gather | bytes 557056 | tf_op jit(solution)/shard_map/all_gather | solution.py:130
  36.7 0.1 slice.62
  36.9 0.2 pad.4.beam_ref
  37.1 0.1 convert_element_type.37
  37.2 1.4 %and_reduce_fusion = (pred[65536]{0:T(1024)(128)(4,1)S(1)}, s32[1,65536]{1,0:T(1,128)S(1)}) fusion(s32[]{:T(128)S(6)} %add.48, s32[]{:T(128)} %mul.78, f32[4,65536]{1,0:T(4,128)S(1)} %convert_element_type.37), kind=kLoop, calls=%fused_computation.8 | loop fusion | flops 393216 | bytes 851976 | tf_op jit(solution)/shard_map/and | solution.py:138
  38.6 0.1 reduce_or.9
  38.8 0.2 convert_reduce_fusion
  38.9 0.2 select_reduce_fusion
  39.1 0.1 convert_reduce_fusion.1.count_ref
  39.2 71.9 %shard_map.46 = f32[2048,128]{1,0:T(8,128)S(1)} custom-call(s32[512]{0:T(512)S(1)} %bitcast.22, s32[2]{0:T(128)S(1)} %convert_reduce_fusion.1.count_ref, s32[1]{0:T(128)} %bitcast.5.base_ref, f32[2,67712]{1,0:T(2,128)S(1)} %pad.4.beam_ref, s32[1,65536]{1,0:T(1,128)S(1)} %get-tuple-element.6.bins_ref), custom_call_target="tpu_custom_call" | custom-call | tf_op jit(solution)/shard_map/pallas_call | solution.py:146
  111.1 1.0 multiply_add_fusion
  112.1 0.3 reduce-precision_convert_fusion
  112.5 2.4 %fusion.1 = f32[2048,256]{0,1:T(8,128)S(1)} fusion(bf16[2048,2048]{1,0:T(8,128)(2,1)S(1)} %copy-done.1, bf16[2048,128]{1,0:T(8,128)(2,1)S(1)} %get-tuple-element.8, bf16[2048,128]{1,0:T(8,128)(2,1)S(1)} %get-tuple-element.7), kind=kOutput, calls=%fused_computation.9 | convolution fusion | flops 2149580800 | bytes 11534336 | tf_op jit(solution)/shard_map/dot_general | solution.py:167
  114.9 0.1 slice_add_fusion
  115.0 0.1 fusion.4
  115.1 0.8 maximum_multiply_fusion
  (8 shorter events, 0.1 us)
Async XLA Ops:
  0.0 1.0 copy-start
  39.2 73.3 %copy-start.1 = (bf16[2048,2048]{1,0:T(8,128)(2,1)S(1)}, bf16[2048,2048]{1,0:T(8,128)(2,1)}, u32[]{:S(2)}) copy-start(bf16[2048,2048]{1,0:T(8,128)(2,1)} %constant.64.clone) | copy-start | bytes 25165828

commit v3 on v2

--- a/solution.py
+++ b/solution.py
@@ -29,7 +29,7 @@
     return jnp.dot(mixer_rows, flat_volts, preferred_element_type=jnp.float32)
 
 
-def fold_kernel(chunk, bin_count, list_ref, count_ref, base_ref, beam_ref, bins_ref, out_ref, shifted, hankel):
+def fold_kernel(chunk, bin_count, list_ref, count_ref, base_ref, beam_ref, bins_ref, out_ref, shifted, hankel, total):
     step = pl.program_id(0)
     start = pl.multiple_of(step * chunk, BLOCK)
     width = chunk + LAGS
@@ -37,7 +37,8 @@
 
     @pl.when(step == 0)
     def _():
-        out_ref[...] = jnp.zeros_like(out_ref)
+        total[...] = jnp.zeros_like(total)
+        shifted[:, :, width:] = jnp.zeros((2, GROUP, BLOCK), jnp.float32)
 
     count = count_ref[step]
 
@@ -84,31 +85,44 @@
         lax.fori_loop(0, width // (UNROLL * BLOCK), build, 0)
         target = base_ref[0] + lax.broadcasted_iota(jnp.int32, (bin_count, BLOCK), 0)
 
-        def fold(position, carry):
-            row_start = pl.multiple_of(list_ref[step * blocks_here + position] * BLOCK, BLOCK)
-            lane = pl.ds(pl.multiple_of(start + row_start, BLOCK), BLOCK)
+        def chosen_rows(lane, wanted):
             real = beam_ref[0:1, lane]
             imag = beam_ref[1:2, lane]
-            chosen = bins_ref[0:1, lane] == target
+            chosen = bins_ref[0:1, lane] == wanted
             zero = jnp.zeros((bin_count, BLOCK), jnp.float32)
             chosen_real = jnp.where(chosen, real, zero)
             chosen_imag = jnp.where(chosen, imag, zero)
+            return [
+                jnp.concatenate([chosen_real, chosen_imag], 1),
+                jnp.concatenate([-chosen_imag, chosen_real], 1),
+            ]
+
+        def fold(position, carry):
+            block = list_ref[step * blocks_here + position]
+            row_start = pl.multiple_of(block * BLOCK, BLOCK)
+            lane = pl.multiple_of(start + row_start, BLOCK)
+            inside = block + 1 < blocks_here
+            after = pl.multiple_of(jnp.where(inside, lane + BLOCK, lane), BLOCK)
             right = jnp.concatenate(
-                [
-                    jnp.concatenate([chosen_real, chosen_imag], 1),
-                    jnp.concatenate([-chosen_imag, chosen_real], 1),
-                ],
+                chosen_rows(pl.ds(lane, BLOCK), target)
+                + chosen_rows(pl.ds(after, BLOCK), jnp.where(inside, target, -1)),
                 0,
             ).astype(jnp.bfloat16)
-            for piece in range(LAGS // LAG_PIECE):
-                rows = pl.ds(piece * LAG_PIECE, LAG_PIECE)
-                left = hankel[pl.ds(pl.multiple_of(row_start + piece * LAG_PIECE, BLOCK), LAG_PIECE), :]
-                out_ref[rows, :] += lax.dot_general(
+            first = 0
+            while first < LAGS + BLOCK:
+                size = min(LAG_PIECE, LAGS + BLOCK - first)
+                left = hankel[pl.ds(pl.multiple_of(row_start + first, BLOCK), size), :]
+                total[pl.ds(first, size), :] += lax.dot_general(
                     left, right, (((1,), (1,)), ((), ())), preferred_element_type=jnp.float32
                 )
+                first += size
             return carry
 
         lax.fori_loop(0, count, fold, 0)
+
+    @pl.when(step == pl.num_programs(0) - 1)
+    def _():
+        out_ref[...] = total[:LAGS, : 2 * bin_count] + total[BLOCK:, 2 * bin_count :]
 
 
 def transform_table(row_count):
@@ -138,6 +152,9 @@
     inside = (all_bins >= base) & (all_bins < base + own_bins)
     touched = jnp.any(inside.reshape(steps, here, BLOCK), axis=2)
     number = jnp.arange(here, dtype=jnp.int32)
+    gap = ~touched[:, None, :] & (number[None, None, :] < number[None, :, None])
+    last_gap = jnp.max(jnp.where(gap, number[None, None, :], -1), 2)
+    touched = touched & ((number[None, :] - last_gap) % 2 == 1)
     before = jnp.sum(touched[:, None, :] & (number[None, None, :] < number[None, :, None]), 2, dtype=jnp.int32)
     counts = jnp.sum(touched, 1, dtype=jnp.int32)
     hit = touched[:, None, :] & (before[:, None, :] == number[None, :, None])
@@ -152,6 +169,7 @@
         scratch_shapes=[
             pltpu.VMEM((2, GROUP, chunk + LAGS + BLOCK), jnp.float32),
             pltpu.VMEM((chunk + LAGS, 2 * BLOCK), jnp.bfloat16),
+            pltpu.VMEM((LAGS + BLOCK, 4 * bin_count), jnp.float32),
         ],
         compiler_params=pltpu.CompilerParams(vmem_limit_bytes=48 * 2**20),
     )(listed.reshape(-1), counts, base.reshape(1), beam, all_bins.reshape(1, total))

time: 116 us -> 104 us (0.90)
  Pallas kernels: 71.9 us -> 59.3 us
    pallas_call x1, Pallas kernels: 71.9 us -> 59.3 us  [per_device(): pl.pallas_call(functools.partial(fold_kernel, chunk, bin_count), grid=(st...]
where the time goes in v3:
time: 104 us
  Pallas kernels  59.3 us (57%)
  blocking collectives  33.1 us (32%)
  other arithmetic  6.3 us (6%)
  matrix products  2.55 us (2%)
  local copies, waits for them, and re-layouts  2.13 us (2%)
    pallas_call x1, Pallas kernels, per_device(): pl.pallas_call(functools.partial(fold_kernel, chunk, bin_count), grid=(st...  59.3 us
    all_gather x1, blocking collectives, per_device(): lax.all_gather(jnp.concatenate([beam, digits], 0), 'tm', axis=1, tiled=True)  23.1 us
    psum x1, blocking collectives, per_device(): lax.psum(form_beam(voltages, beam_weights), 'dish').astype(jnp.bfloat16)  9.95 us
    dot_general x1, matrix products, per_device(): product = jnp.dot(table, split, preferred_element_type=jnp.float32)  2.37 us

profile of v3, /device:TPU:0, one launch (start us, length us, event | category | flops | bytes accessed | tf_op | source)
XLA Modules:
  0.0 103.5 jit_solution(9944997983199637434)
XLA Ops:
  0.0 1.0 %copy-done = bf16[2,32,4096]{2,1,0:T(8,128)(2,1)S(1)} copy-done((bf16[2,32,4096]{2,1,0:T(8,128)(2,1)S(1)}, bf16[2,32,4096]{2,1,0:T(8,128)(2,1)}, u32[]{:S(2)}) %copy-start) | copy-done | bytes 524312
  1.0 0.7 fusion.25
  1.7 0.7 slice_bitcast_fusion
  2.4 0.1 maximum_bitcast_fusion
  2.6 0.7 fusion.6
  3.4 0.2 fusion.19
  3.5 10.0 %psum.7 = bf16[2,4096]{1,0:T(2,128)(2,1)S(1)} all-reduce(f32[2,4096]{1,0:T(2,128)S(1)} %fusion.19), channel_id=1, replica_groups=mesh['tm'=16,'dish'=2] {'dish'}, use_global_device_ids=true, to_apply=%region_0.1 | all-reduce | flops 8192 | bytes 49152 | tf_op jit(solution)/shard_map/psum | solution.py:143
  13.6 23.1 %all_gather.3 = bf16[4,65536]{1,0:T(4,128)(2,1)S(1)} all-gather(bf16[4,4096]{1,0:T(4,128)(2,1)S(1)} %pad_maximum_fusion.3), channel_id=1, replica_groups=mesh['tm'=16,'dish'=2] {'tm'}, dimensions={1}, use_global_device_ids=true | all-gather | bytes 557056 | tf_op jit(solution)/shard_map/all_gather | solution.py:144
  36.7 0.1 slice.62
  36.9 0.2 pad.4.beam_ref
  37.1 0.1 convert_element_type.37
  37.2 1.4 %and_reduce_fusion = (pred[65536]{0:T(1024)(128)(4,1)S(1)}, s32[1,65536]{1,0:T(1,128)S(1)}) fusion(s32[]{:T(128)S(6)} %add.58, s32[]{:T(128)} %mul.78, f32[4,65536]{1,0:T(4,128)S(1)} %convert_element_type.37), kind=kLoop, calls=%fused_computation.8 | loop fusion | flops 393216 | bytes 851976 | tf_op jit(solution)/shard_map/and | solution.py:152
  38.6 0.1 reduce_or.9
  38.8 0.2 select_reduce_fusion.1
  38.9 0.1 convert_reduce_fusion.1
  39.1 0.1 convert_reduce_fusion
  39.2 0.2 select_reduce_fusion
  39.4 59.3 %shard_map.46 = f32[2048,128]{1,0:T(8,128)S(1)} custom-call(s32[512]{0:T(512)S(1)} %bitcast.22, s32[2]{0:T(128)S(1)} %get-tuple-element.5.count_ref, s32[1]{0:T(128)} %bitcast.5.base_ref, f32[2,67712]{1,0:T(2,128)S(1)} %pad.4.beam_ref, s32[1,65536]{1,0:T(1,128)S(1)} %get-tuple-element.8.bins_ref), custom_call_target="tpu_custom_call" | custom-call | tf_op jit(solution)/shard_map/pallas_call | solution.py:163
  98.8 1.0 multiply_add_fusion
  99.8 0.3 reduce-precision_convert_fusion
  100.1 2.4 %fusion.1 = f32[2048,256]{0,1:T(8,128)S(1)} fusion(bf16[2048,2048]{1,0:T(8,128)(2,1)S(1)} %copy-done.1, bf16[2048,128]{1,0:T(8,128)(2,1)S(1)} %get-tuple-element.10, bf16[2048,128]{1,0:T(8,128)(2,1)S(1)} %get-tuple-element.9), kind=kOutput, calls=%fused_computation.9 | convolution fusion | flops 2149580800 | bytes 11534336 | tf_op jit(solution)/shard_map/dot_general | solution.py:185
  102.5 0.1 slice_add_fusion
  102.6 0.1 fusion.4
  102.7 0.8 maximum_multiply_fusion
  (10 shorter events, 0.2 us)
Async XLA Ops:
  0.0 1.0 %copy-start = (bf16[2,32,4096]{2,1,0:T(8,128)(2,1)S(1)}, bf16[2,32,4096]{2,1,0:T(8,128)(2,1)}, u32[]{:S(2)}) copy-start(bf16[2,32,4096]{2,1,0:T(8,128)(2,1)} %param.4) | copy-start | bytes 1572868
  39.4 60.7 %copy-start.1 = (bf16[2048,2048]{1,0:T(8,128)(2,1)S(1)}, bf16[2048,2048]{1,0:T(8,128)(2,1)}, u32[]{:S(2)}) copy-start(bf16[2048,2048]{1,0:T(8,128)(2,1)} %constant.78.clone) | copy-start | bytes 25165828

commit v4 on v3

--- a/solution.py
+++ b/solution.py
@@ -27,6 +27,74 @@
     )
     flat_volts = volt_block.reshape(2 * dish_count, volt_block.shape[2])
     return jnp.dot(mixer_rows, flat_volts, preferred_element_type=jnp.float32)
+
+
+def gather_kernel(count_tm, count_dish, part_ref, digit_ref, out_ref, arrived, sem_part, sem_block):
+    me = lax.axis_index("tm")
+    mine = lax.axis_index("dish")
+    barrier = pltpu.get_barrier_semaphore()
+    for away in range(1, count_tm):
+        pl.semaphore_signal(
+            barrier, inc=1, device_id={"tm": lax.rem(me + away, count_tm)}, device_id_type=pl.DeviceIdType.MESH
+        )
+    for away in range(1, count_dish):
+        pl.semaphore_signal(
+            barrier, inc=1, device_id={"dish": lax.rem(mine + away, count_dish)}, device_id_type=pl.DeviceIdType.MESH
+        )
+    pl.semaphore_wait(barrier, count_tm + count_dish - 2)
+    copies = []
+    for away in range(1, count_dish):
+        copy = pltpu.make_async_remote_copy(
+            src_ref=part_ref,
+            dst_ref=arrived.at[away - 1],
+            send_sem=sem_part.at[0, away - 1],
+            recv_sem=sem_part.at[1, away - 1],
+            device_id={"dish": lax.rem(mine + away, count_dish)},
+            device_id_type=pl.DeviceIdType.MESH,
+        )
+        copy.start()
+        copies.append(copy)
+    rows = part_ref.shape[0]
+    out_ref[me, rows:, :] = digit_ref[...]
+    beam = part_ref[...]
+    for away, copy in enumerate(copies):
+        copy.wait()
+        beam = beam + arrived[away]
+    out_ref[me, :rows, :] = beam.astype(jnp.bfloat16)
+    copies = []
+    for away in range(1, count_tm):
+        copy = pltpu.make_async_remote_copy(
+            src_ref=out_ref.at[me],
+            dst_ref=out_ref.at[me],
+            send_sem=sem_block.at[0, away - 1],
+            recv_sem=sem_block.at[1, away - 1],
+            device_id={"tm": lax.rem(me + away, count_tm)},
+            device_id_type=pl.DeviceIdType.MESH,
+        )
+        copy.start()
+        copies.append(copy)
+    for copy in copies:
+        copy.wait()
+
+
+def gather_beam(partial, digits, count_tm, count_dish):
+    rows = partial.size // BLOCK
+    blocks = pl.pallas_call(
+        functools.partial(gather_kernel, count_tm, count_dish),
+        out_shape=jax.ShapeDtypeStruct((count_tm, 2 * rows, BLOCK), jnp.bfloat16),
+        in_specs=[pl.BlockSpec(memory_space=pltpu.VMEM)] * 2,
+        out_specs=pl.BlockSpec(memory_space=pltpu.VMEM),
+        scratch_shapes=[
+            pltpu.VMEM((max(1, count_dish - 1), rows, BLOCK), jnp.float32),
+            pltpu.SemaphoreType.DMA((2, max(1, count_dish - 1))),
+            pltpu.SemaphoreType.DMA((2, max(1, count_tm - 1))),
+        ],
+        compiler_params=pltpu.CompilerParams(
+            collective_id=0, has_side_effects=True, vmem_limit_bytes=16 * 2**20
+        ),
+    )(partial.reshape(rows, BLOCK), digits.reshape(rows, BLOCK))
+    samples = partial.shape[1]
+    return jnp.swapaxes(blocks.reshape(count_tm, 4, samples), 0, 1).reshape(4, count_tm * samples)
 
 
 def fold_kernel(chunk, bin_count, list_ref, count_ref, base_ref, beam_ref, bins_ref, out_ref, shifted, hankel, total):
@@ -140,8 +208,7 @@
     bin_count = max(own_bins, 64)
     base = lax.axis_index("tm") * own_bins
     digits = jnp.stack([phase_bins // DIGIT, phase_bins % DIGIT]).astype(jnp.bfloat16)
-    beam = lax.psum(form_beam(voltages, beam_weights), "dish").astype(jnp.bfloat16)
-    gathered = lax.all_gather(jnp.concatenate([beam, digits], 0), "tm", axis=1, tiled=True)
+    gathered = gather_beam(form_beam(voltages, beam_weights), digits, count_tm, count_dish)
     gathered = gathered.astype(jnp.float32)
     beam = jnp.pad(gathered[:2], ((0, 0), (0, LAGS + BLOCK)))
     all_bins = (gathered[2] * DIGIT + gathered[3]).astype(jnp.int32)

time: 104 us -> 93.7 us (0.901); the launches traced: 104 us -> 92 us
  blocking collectives: 33.1 us -> 0 us
  Pallas kernels: 59.3 us -> 77.1 us
  matrix products: 2.55 us -> 5.94 us
  local copies, waits for them, and re-layouts: 2.13 us -> 3.81 us
  other arithmetic: 6.3 us -> 4.89 us
    all_gather x1 -> x0, blocking collectives: 23.1 us -> none  [per_device(): lax.all_gather(jnp.concatenate([beam, digits], 0), 'tm', axis=1, tiled=True)]
    pallas_call x0 -> x1, Pallas kernels: none -> 17.8 us  [gather_beam(): pl.pallas_call(functools.partial(gather_kernel, count_tm, count_dish), ou...]
    psum x1 -> x0, blocking collectives: 9.95 us -> none  [per_device(): lax.psum(form_beam(voltages, beam_weights), 'dish').astype(jnp.bfloat16)]
    dot_general x1, matrix products: 2.37 us -> 5.76 us  [per_device(): product = jnp.dot(table, split, preferred_element_type=jnp.float32)]
    and x1, other arithmetic: 1.41 us -> 0.1 us  [per_device(): inside = (all_bins >= base) & (all_bins < base + own_bins)]
where the time goes in v4:
time: 93.7 us; the launch traced here: 92 us
  Pallas kernels  77.1 us (82%)
  matrix products  5.94 us (6%)
  other arithmetic  4.89 us (5%)
  local copies, waits for them, and re-layouts  3.81 us (4%)
    pallas_call x1, Pallas kernels, per_device(): pl.pallas_call(functools.partial(fold_kernel, chunk, bin_count), grid=(st...  59.3 us
    pallas_call x1, Pallas kernels, gather_beam(): pl.pallas_call(functools.partial(gather_kernel, count_tm, count_dish), ou...  17.8 us
    dot_general x1, matrix products, per_device(): product = jnp.dot(table, split, preferred_element_type=jnp.float32)  5.76 us

profile of v4, /device:TPU:0, one launch (start us, length us, event | category | flops | bytes accessed | tf_op | source)
XLA Modules:
  0.0 92.0 jit_solution(16077711281788042535)
XLA Ops:
  0.0 1.0 %copy-done = bf16[2,32,4096]{2,1,0:T(8,128)(2,1)S(1)} copy-done((bf16[2,32,4096]{2,1,0:T(8,128)(2,1)S(1)}, bf16[2,32,4096]{2,1,0:T(8,128)(2,1)}, u32[]{:S(2)}) %copy-start) | copy-done | bytes 524312
  1.0 0.7 fusion.26
  1.7 0.7 slice_bitcast_fusion.1
  2.4 0.1 maximum_bitcast_fusion
  2.6 0.7 fusion.7
  3.4 0.2 fusion.20
  3.7 17.8 %shard_map.46 = bf16[16,128,128]{2,1,0:T(8,128)(2,1)S(1)} custom-call(f32[64,128]{1,0:T(8,128)S(1)} %reshape.104.part_ref, bf16[64,128]{1,0:T(8,128)(2,1)S(1)} %convert_element_type.49.digit_ref), custom_call_target="tpu_custom_call" | custom-call | tf_op jit(solution)/shard_map/pallas_call | solution.py:82
  21.5 0.4 reshape.112
  21.9 0.6 copy.11
  22.5 0.1 compare_and_fusion
  22.7 0.1 reduce_or.9
  22.9 0.2 select_reduce_fusion.1
  23.0 0.1 convert_reduce_fusion.1
  23.2 0.1 convert_reduce_fusion
  23.3 0.2 select_reduce_fusion
  23.6 0.4 copy.8
  24.0 0.3 copy.9
  24.3 0.2 pad.4.beam_ref
  24.5 59.3 %shard_map.47 = f32[2048,128]{1,0:T(8,128)S(1)} custom-call(s32[512]{0:T(512)S(1)} %bitcast.31, s32[2]{0:T(128)S(1)} %get-tuple-element.5.count_ref, s32[1]{0:T(128)} %bitcast.6.base_ref, f32[2,67712]{1,0:T(2,128)S(1)} %pad.4.beam_ref, s32[1,65536]{1,0:T(1,128)S(1)} %bitcast.30), custom_call_target="tpu_custom_call" | custom-call | tf_op jit(solution)/shard_map/pallas_call | solution.py:230
  83.8 1.0 %multiply_add_fusion = (f32[2048,64]{1,0:T(8,128)S(1)}, f32[2048,64]{1,0:T(8,128)S(1)}) fusion(f32[2048,128]{1,0:T(8,128)S(1)} %shard_map.47, f32[2048]{0:T(1024)S(1)} %get-tuple-element.19, f32[2048]{0:T(1024)S(1)} %get-tuple-element.20), kind=kLoop, calls=%fused_computation.8 | loop fusion | flops 786432 | bytes 2113536 | tf_op jit(solution)/shard_map/add | solution.py:249
  84.8 0.3 reduce-precision_convert_fusion
  85.1 5.8 %fusion.1 = f32[2048,256]{0,1:T(8,128)S(1)} fusion(bf16[2048,2048]{1,0:T(8,128)(2,1)} %constant.78.clone, bf16[2048,128]{1,0:T(8,128)(2,1)S(1)} %get-tuple-element.8, bf16[2048,128]{1,0:T(8,128)(2,1)S(1)} %get-tuple-element.7), kind=kOutput, calls=%fused_computation.9 | convolution fusion | flops 2149580800 | bytes 11534336 | tf_op jit(solution)/shard_map/dot_general | solution.py:252
  90.9 0.1 slice_add_fusion
  91.1 0.8 maximum_multiply_fusion
  (14 shorter events, 0.4 us)
Async XLA Ops:
  0.0 1.0 %copy-start = (bf16[2,32,4096]{2,1,0:T(8,128)(2,1)S(1)}, bf16[2,32,4096]{2,1,0:T(8,128)(2,1)}, u32[]{:S(2)}) copy-start(bf16[2,32,4096]{2,1,0:T(8,128)(2,1)} %param.4) | copy-start | bytes 1572868

commit v5 on v4

--- a/solution.py
+++ b/solution.py
@@ -112,22 +112,25 @@
 
     @pl.when(count > 0)
     def _():
-        row = lax.broadcasted_iota(jnp.int32, (GROUP, SPAN + BLOCK), 0)
+        half = GROUP // 2
+        row = lax.broadcasted_iota(jnp.int32, (half, SPAN + BLOCK), 0)
 
         def shift_rows(position, carry):
             lane = pl.multiple_of(position * SPAN, SPAN)
             for part in range(2):
                 rows = jnp.broadcast_to(
                     beam_ref[pl.ds(part, 1), pl.ds(pl.multiple_of(start + lane, BLOCK), SPAN + BLOCK)],
-                    (GROUP, SPAN + BLOCK),
+                    (half, SPAN + BLOCK),
                 )
                 amount = 1
-                while amount < GROUP:
+                while amount < half:
                     rows = jnp.where(
                         (row & amount) != 0, pltpu.roll(rows, SPAN + BLOCK - amount, 1), rows
                     )
                     amount *= 2
-                shifted[part, :, pl.ds(lane, SPAN)] = rows[:, :SPAN]
+                later = pltpu.roll(rows, SPAN + BLOCK - half, 1)
+                shifted[part, :half, pl.ds(lane, SPAN)] = rows[:, :SPAN]
+                shifted[part, half:, pl.ds(lane, SPAN)] = later[:, :SPAN]
             return carry
 
         lax.fori_loop(0, width // SPAN, shift_rows, 0)

time: 93.7 us -> 93.7 us (level)
  no operation moved by 1% of the time
where the time goes in v5:
time: 93.7 us; the launch traced here: 92 us
  Pallas kernels  77.1 us (82%)
  matrix products  5.94 us (6%)
  other arithmetic  4.89 us (5%)
  local copies, waits for them, and re-layouts  3.81 us (4%)
    pallas_call x1, Pallas kernels, per_device(): pl.pallas_call(functools.partial(fold_kernel, chunk, bin_count), grid=(st...  59.3 us
    pallas_call x1, Pallas kernels, gather_beam(): pl.pallas_call(functools.partial(gather_kernel, count_tm, count_dish), ou...  17.8 us
    dot_general x1, matrix products, per_device(): product = jnp.dot(table, split, preferred_element_type=jnp.float32)  5.76 us

profile of v5, /device:TPU:0, one launch (start us, length us, event | category | flops | bytes accessed | tf_op | source)
XLA Modules:
  0.0 92.0 jit_solution(10113222363099978890)
XLA Ops:
  0.0 1.0 %copy-done = bf16[2,32,4096]{2,1,0:T(8,128)(2,1)S(1)} copy-done((bf16[2,32,4096]{2,1,0:T(8,128)(2,1)S(1)}, bf16[2,32,4096]{2,1,0:T(8,128)(2,1)}, u32[]{:S(2)}) %copy-start) | copy-done | bytes 524312
  1.0 0.7 fusion.26
  1.7 0.7 slice_bitcast_fusion.1
  2.4 0.1 maximum_bitcast_fusion
  2.6 0.7 fusion.7
  3.4 0.2 fusion.20
  3.7 17.8 %shard_map.46 = bf16[16,128,128]{2,1,0:T(8,128)(2,1)S(1)} custom-call(f32[64,128]{1,0:T(8,128)S(1)} %reshape.104.part_ref, bf16[64,128]{1,0:T(8,128)(2,1)S(1)} %convert_element_type.49.digit_ref), custom_call_target="tpu_custom_call" | custom-call | tf_op jit(solution)/shard_map/pallas_call | solution.py:82
  21.5 0.4 reshape.112
  21.9 0.6 copy.11
  22.5 0.1 compare_and_fusion
  22.7 0.1 reduce_or.9
  22.9 0.2 select_reduce_fusion.1
  23.0 0.1 convert_reduce_fusion.1
  23.2 0.1 convert_reduce_fusion
  23.3 0.2 select_reduce_fusion
  23.6 0.4 copy.8
  24.0 0.3 copy.9
  24.3 0.2 pad.4.beam_ref
  24.5 59.3 %shard_map.47 = f32[2048,128]{1,0:T(8,128)S(1)} custom-call(s32[512]{0:T(512)S(1)} %bitcast.31, s32[2]{0:T(128)S(1)} %get-tuple-element.5.count_ref, s32[1]{0:T(128)} %bitcast.6.base_ref, f32[2,67712]{1,0:T(2,128)S(1)} %pad.4.beam_ref, s32[1,65536]{1,0:T(1,128)S(1)} %bitcast.30), custom_call_target="tpu_custom_call" | custom-call | tf_op jit(solution)/shard_map/pallas_call | solution.py:233
  83.8 1.0 %multiply_add_fusion = (f32[2048,64]{1,0:T(8,128)S(1)}, f32[2048,64]{1,0:T(8,128)S(1)}) fusion(f32[2048,128]{1,0:T(8,128)S(1)} %shard_map.47, f32[2048]{0:T(1024)S(1)} %get-tuple-element.19, f32[2048]{0:T(1024)S(1)} %get-tuple-element.20), kind=kLoop, calls=%fused_computation.8 | loop fusion | flops 786432 | bytes 2113536 | tf_op jit(solution)/shard_map/add | solution.py:252
  84.8 0.3 reduce-precision_convert_fusion
  85.1 5.8 %fusion.1 = f32[2048,256]{0,1:T(8,128)S(1)} fusion(bf16[2048,2048]{1,0:T(8,128)(2,1)} %constant.78.clone, bf16[2048,128]{1,0:T(8,128)(2,1)S(1)} %get-tuple-element.8, bf16[2048,128]{1,0:T(8,128)(2,1)S(1)} %get-tuple-element.7), kind=kOutput, calls=%fused_computation.9 | convolution fusion | flops 2149580800 | bytes 11534336 | tf_op jit(solution)/shard_map/dot_general | solution.py:255
  90.9 0.1 slice_add_fusion
  91.1 0.8 maximum_multiply_fusion
  (14 shorter events, 0.4 us)
Async XLA Ops:
  0.0 1.0 %copy-start = (bf16[2,32,4096]{2,1,0:T(8,128)(2,1)S(1)}, bf16[2,32,4096]{2,1,0:T(8,128)(2,1)}, u32[]{:S(2)}) copy-start(bf16[2,32,4096]{2,1,0:T(8,128)(2,1)} %param.4) | copy-start | bytes 1572868
